TPU v7x, 512 devices: a whole 4x8x8 slice. The times are simulated.
512 devices in a mesh: seq: 64 (over z, x, y_hi), tp: 8 (over y_lo, core).
Axes of the slice: x: 4, y: 8 (y_hi: 2, y_lo: 4; y = y_hi * 4 + y_lo), z: 8, core: 2. Of those that a mesh axis runs over, the one named last changes fastest.
Arguments:
- branches: bfloat16 [3, 16384, 4096], P(None, 'seq', 'tp'), may hold values from -6 to 6
- short_taps: float32 [3, 3, 4096], P(None, None, 'tp'), may hold values from -3 to 3
- skip_gain: float32 [4096], P('tp'), may hold values from -4 to 4
- long_filter: float32 [16384, 4096], P('seq', 'tp'), may hold values from -4 to 4
- out_weight: bfloat16 [4096, 4096], P('seq', 'tp'), may hold values from -0.09375 to 0.09375
Outputs:
- block_out: bfloat16 [16384, 4096], P('seq', 'tp')
All inputs are finite; a program needn't handle non-finite values.
Results may differ from a plain program's by a relative error of at most 0.0049.
Values may be sent and summed in bfloat16 or wider, within the bound.
A program may use at most 64 MiB of HBM per device.

v0:
```python
import functools
import math

import jax
import jax.numpy as jnp
from jax import lax
from jax.experimental import pallas as pl
from jax.experimental.pallas import tpu as pltpu
from jax.sharding import PartitionSpec as P

MESH = pl.DeviceIdType.MESH
LANES = 128
GROUP = 8
SHIFTS = 16


def ring_sizes(seq_size):
    return (seq_size // 8, 4, 2) if seq_size >= 32 else (seq_size // 4, 2, 2)


def place(seq_size):
    nz, nx, ny = ring_sizes(seq_size)
    me = lax.axis_index("seq")
    return me // (nx * ny), (me // ny) % nx, me % ny


def remote(src, dst, send_sem, recv_sem, device_id):
    return pltpu.make_async_remote_copy(
        src_ref=src,
        dst_ref=dst,
        send_sem=send_sem,
        recv_sem=recv_sem,
        device_id=device_id,
        device_id_type=MESH,
    )


def scatter_start(send, land, send_sem, recv_sem):
    count = send.shape[0]
    me = lax.axis_index("seq")

    def step(t, carry):
        peer = lax.rem(me + t, count)
        remote(send.at[peer], land.at[me], send_sem, recv_sem, {"seq": peer}).start()
        return carry

    lax.fori_loop(1, count, step, 0)
    land[me] = send[me]


def scatter_wait(send, land, send_sem, recv_sem):
    others = pl.ds(0, send.shape[0] - 1)
    copy = remote(send.at[others], land.at[others], send_sem, recv_sem, {"seq": 0})
    copy.wait_recv()
    return copy


def pack_rows(block_of, halves, send, column, width):
    parts = [block_of(h).T.reshape(width // GROUP, GROUP, LANES) for h in range(halves)]
    send[pl.ds(column // GROUP, width // GROUP)] = jnp.concatenate(parts, axis=1).astype(send.dtype)


def unpack_channels(land, wide, out):
    wide[...] = land[...].astype(jnp.float32).reshape(wide.shape)
    blocks = out.shape[1]
    for j in range(GROUP):
        out[j] = wide[pl.ds(j, blocks, stride=GROUP), :]


def front_kernel(
    branches, taps, gain, long_filter, weight,
    gate_out, direct_out, signal_out, filter_out, weight_a_out, weight_b_out,
    halo, extended, send_f, send_s, land_f, land_s, wide, weight_a, weight_b,
    halo_sems, a2a_sems, y_sems, x_send, x_recv, z_send, z_recv,
):
    seq_size = land_f.shape[0]
    nz, nx, ny = ring_sizes(seq_size)
    z, x, y = place(seq_size)
    me = lax.axis_index("seq")
    rows, channels = long_filter.shape
    halves = rows // LANES
    width = min(LANES, channels)
    half_columns = weight_a.shape[-1]

    following = lax.rem(me + 1, seq_size)
    halo_copy = remote(
        branches.at[:, pl.ds(rows - 16, 16), :], halo, halo_sems.at[0], halo_sems.at[1], {"seq": following}
    )
    halo_copy.start()
    weight_a[x, y] = weight[:, :half_columns]
    weight_b[z, y] = weight[:, half_columns:]
    other_y = me + 1 - 2 * y
    y_a = remote(weight_a.at[x, y], weight_a.at[x, y], y_sems.at[0], y_sems.at[1], {"seq": other_y})
    y_b = remote(weight_b.at[z, y], weight_b.at[z, y], y_sems.at[2], y_sems.at[3], {"seq": other_y})
    y_a.start()
    y_b.start()

    for column in range(0, channels, width):
        pack_rows(
            lambda h: long_filter[h * LANES : (h + 1) * LANES, column : column + width],
            halves, send_f, column, width,
        )
    scatter_start(send_f, land_f, a2a_sems.at[0], a2a_sems.at[1])

    halo_copy.wait()
    first = me == 0
    for column in range(0, channels, width):
        span = slice(column, column + width)
        mixed = []
        for branch in range(3):
            before = halo[branch, :, span].astype(jnp.float32)
            extended[branch, 0:16, :] = jnp.where(first, 0.0, before)
            extended[branch, 16:, :] = branches[branch, :, span].astype(jnp.float32)
            total = taps[0, branch : branch + 1, span] * extended[branch, 16 : 16 + rows, :]
            for lag in (1, 2):
                total += taps[lag, branch : branch + 1, span] * extended[branch, 16 - lag : 16 - lag + rows, :]
            mixed.append(total)
        signal = mixed[1] * mixed[2]
        gate_out[:, span] = mixed[0]
        direct_out[:, span] = gain[0:1, span] * signal
        pack_rows(lambda h: signal[h * LANES : (h + 1) * LANES], halves, send_s, column, width)
    scatter_start(send_s, land_s, a2a_sems.at[2], a2a_sems.at[3])

    y_a.wait()
    y_b.wait()
    x_copies = []
    for t in range(1, nx):
        peer_x = lax.rem(x + t, nx)
        copy = remote(
            weight_a.at[x], weight_a.at[x], x_send.at[t], x_recv.at[x], {"seq": (z * nx + peer_x) * ny + y}
        )
        copy.start()
        x_copies.append(copy)
    z_copies = []
    for t in range(1, nz):
        peer_z = lax.rem(z + t, nz)
        copy = remote(
            weight_b.at[z], weight_b.at[z], z_send.at[t], z_recv.at[z], {"seq": (peer_z * nx + x) * ny + y}
        )
        copy.start()
        z_copies.append(copy)

    copy_f = scatter_wait(send_f, land_f, a2a_sems.at[0], a2a_sems.at[1])
    unpack_channels(land_f, wide, filter_out)
    copy_s = scatter_wait(send_s, land_s, a2a_sems.at[2], a2a_sems.at[3])
    unpack_channels(land_s, wide, signal_out)
    for t in range(1, nx):
        source = lax.rem(x + nx - t, nx)
        remote(weight_a.at[source], weight_a.at[source], x_send.at[t], x_recv.at[source], {"seq": me}).wait_recv()
    for t in range(1, nz):
        source = lax.rem(z + nz - t, nz)
        remote(weight_b.at[source], weight_b.at[source], z_send.at[t], z_recv.at[source], {"seq": me}).wait_recv()
    weight_a_out[...] = weight_a[...]
    weight_b_out[...] = weight_b[...]
    copy_f.wait_send()
    copy_s.wait_send()
    for copy in x_copies + z_copies:
        copy.wait_send()


def convolve_kernel(scale, signal, long_filter, out, padded, taps, shifted, total, wide):
    blocks = signal.shape[1]
    step = min(2 * SHIFTS, blocks)
    padded[0:SHIFTS, :] = jnp.zeros((SHIFTS, LANES), jnp.float32)
    taps[0:8, :] = jnp.zeros((8, LANES), jnp.float32)
    row = lax.broadcasted_iota(jnp.int32, (LANES, LANES), 0)
    lane = lax.broadcasted_iota(jnp.int32, (LANES, LANES), 1)
    causal = lane >= row

    def rolled(block):
        line = jnp.broadcast_to(taps[8 + block : 9 + block, :], (LANES, LANES))
        return pltpu.roll(line, 0, 1, stride=1, stride_axis=0)

    def channel(j, carry):
        padded[SHIFTS:, :] = signal[j]
        taps[8:, :] = long_filter[j]
        for shift in range(SHIFTS):
            shifted[:, shift * LANES : (shift + 1) * LANES] = padded[
                SHIFTS - shift : SHIFTS - shift + blocks, :
            ].astype(jnp.bfloat16)
        for start in range(0, blocks, step):
            height = blocks - start
            spans = range(start, min(start + step, blocks), SHIFTS)
            last = [rolled(span - 1) for span in spans]
            partial = None
            for shift in range(0, SHIFTS, 2):
                tiles = []
                for extra in range(2):
                    here = [rolled(span + shift + extra) for span in spans]
                    tiles.append(
                        jnp.concatenate(
                            [jnp.where(causal, h, b).astype(jnp.bfloat16) for h, b in zip(here, last)], axis=1
                        )
                    )
                    last = here
                term = jnp.dot(
                    shifted[0:height, shift * LANES : (shift + 2) * LANES],
                    jnp.concatenate(tiles, axis=0),
                    preferred_element_type=jnp.float32,
                )
                partial = term if partial is None else partial + term
            if start == 0:
                total[...] = partial[:, :LANES]
            else:
                total[start:, :] += partial[:, :LANES]
            if len(spans) > 1:
                total[start + SHIFTS :, :] += partial[: height - SHIFTS, LANES:]
        wide[:, pl.ds(j, 1), :] = (total[...] * scale).reshape(blocks, 1, LANES)
        return carry

    lax.fori_loop(0, GROUP, channel, 0)
    out[...] = wide[...].reshape(out.shape).astype(out.dtype)


def back_kernel(
    convolved, gate, direct, weight_a_in, weight_b_in, out,
    land, gathered, weight_a, weight_b, total,
    a2a_sems, ring_send, ring_recv, x_send, x_recv, tp_send, near_send, tp_recv,
):
    seq_size = land.shape[0]
    nz, nx, ny = ring_sizes(seq_size)
    z, x, y = place(seq_size)
    me = lax.axis_index("seq")
    mine = lax.axis_index("tp")
    tp_size = gathered.shape[0]
    chips = tp_size // 2
    chip, core = mine // 2, mine % 2
    sibling = mine + 1 - 2 * core
    rows, channels = gate.shape
    halves = rows // LANES
    width = min(LANES, channels)

    scatter_start(convolved, land, a2a_sems.at[0], a2a_sems.at[1])
    weight_a[z] = weight_a_in[...]
    weight_b[x] = weight_b_in[...]
    forth = (lax.rem(z + 1, nz) * nx + x) * ny + y
    back = (lax.rem(z + nz - 1, nz) * nx + x) * ny + y
    middle = nx // 2

    def ring_copies(t):
        pair = []
        for way, peer in enumerate((forth, back)):
            block = lax.rem(z + nz - (t - 1), nz) if way == 0 else lax.rem(z + (t - 1), nz)
            piece = weight_a.at[block]
            if 2 * t == nz:
                piece = weight_a.at[block, pl.ds(way * middle, middle)]
            pair.append(remote(piece, piece, ring_send.at[way, t], ring_recv.at[way, t], {"seq": peer}))
        return pair

    ring = {t: ring_copies(t) for t in range(1, nz // 2 + 1)}

    def ring_start(t):
        for copy in ring[t]:
            copy.start()

    def ring_wait(t):
        for copy in ring[t]:
            copy.wait_recv()

    ring_start(1)
    x_copies = []
    for t in range(1, nx):
        peer_x = lax.rem(x + t, nx)
        copy = remote(
            weight_b.at[x], weight_b.at[x], x_send.at[t], x_recv.at[x], {"seq": (z * nx + peer_x) * ny + y}
        )
        copy.start()
        x_copies.append(copy)

    back_copy = scatter_wait(convolved, land, a2a_sems.at[0], a2a_sems.at[1])
    for column in range(0, channels, width):
        slots = pl.ds(column // GROUP, width // GROUP)
        arrived = land[slots].astype(jnp.float32)
        for h in range(halves):
            block = arrived[:, h * GROUP : (h + 1) * GROUP, :].reshape(width, LANES).T
            span = (slice(h * LANES, (h + 1) * LANES), slice(column, column + width))
            gated = gate[span] * (block + direct[span])
            gathered[mine, h * LANES : (h + 1) * LANES, column : column + width] = gated.astype(gathered.dtype)

    own = gathered.at[mine]
    tp_copies = [remote(own, own, near_send.at[0], tp_recv.at[mine], {"tp": sibling})]
    for t in range(1, chips):
        peer = lax.rem(chip + t, chips) * 2 + core
        tp_copies.append(remote(own, own, tp_send.at[t], tp_recv.at[mine], {"tp": peer}))
    for copy in tp_copies:
        copy.start()
    if nz // 2 >= 2:
        ring_wait(1)
        ring_start(2)
    for t in range(1, chips):
        source = lax.rem(chip + chips - t, chips) * 2 + core
        slot = gathered.at[source]
        copy = remote(slot, slot, near_send.at[t], tp_recv.at[source], {"tp": sibling})
        copy.wait_recv()
        copy.start()
        tp_copies.append(copy)
        if t + 2 <= nz // 2:
            ring_wait(t + 1)
            ring_start(t + 2)
    for t in range(0, chips):
        source = lax.rem(chip + chips - t, chips) * 2 + 1 - core
        slot = gathered.at[source]
        remote(slot, slot, near_send.at[t], tp_recv.at[source], {"tp": sibling}).wait_recv()
    ring_wait(nz // 2)
    for t in range(1, nx):
        source = lax.rem(x + nx - t, nx)
        remote(weight_b.at[source], weight_b.at[source], x_send.at[t], x_recv.at[source], {"seq": me}).wait_recv()

    columns = weight_a.shape[-1]
    for part in range(2):
        total[...] = jnp.zeros_like(total)

        def add(block, carry):
            tile = weight_a[block] if part == 0 else weight_b[:, block]
            total[...] += jnp.dot(
                gathered[block], tile.reshape(channels, columns), preferred_element_type=jnp.float32
            )
            return carry

        lax.fori_loop(0, tp_size, add, 0)
        out[:, part * columns : (part + 1) * columns] = total[...].astype(out.dtype)

    back_copy.wait_send()
    for t in ring:
        for copy in ring[t]:
            copy.wait_send()
    for copy in x_copies + tp_copies:
        copy.wait_send()


def vmem(count):
    return [pl.BlockSpec(memory_space=pltpu.VMEM)] * count


def body(seq_size, tp_size, branches, short_taps, skip_gain, long_filter, out_weight):
    rows, channels = long_filter.shape
    weight_rows, columns = out_weight.shape
    nz, nx, ny = ring_sizes(seq_size)
    assert channels == GROUP * seq_size and nz == tp_size and nx * ny * weight_rows == channels
    halves = rows // LANES
    blocks = halves * seq_size
    half = columns // 2
    slots = (seq_size, halves * GROUP, LANES)
    f32, b16 = jnp.float32, jnp.bfloat16
    dma = pltpu.SemaphoreType.DMA
    shape = jax.ShapeDtypeStruct

    gate, direct, signal, filters, weight_a, weight_b = pl.pallas_call(
        front_kernel,
        out_shape=[
            shape((rows, channels), f32),
            shape((rows, channels), f32),
            shape((GROUP, blocks, LANES), f32),
            shape((GROUP, blocks, LANES), f32),
            shape((nx, ny, weight_rows, half), b16),
            shape((nz, ny, weight_rows, half), b16),
        ],
        in_specs=vmem(5),
        out_specs=vmem(6),
        scratch_shapes=[
            pltpu.VMEM((3, 16, channels), b16),
            pltpu.VMEM((3, 16 + rows, min(LANES, channels)), f32),
            pltpu.VMEM(slots, b16),
            pltpu.VMEM(slots, b16),
            pltpu.VMEM(slots, b16),
            pltpu.VMEM(slots, b16),
            pltpu.VMEM((blocks * GROUP, LANES), f32),
            pltpu.VMEM((nx, ny, weight_rows, half), b16),
            pltpu.VMEM((nz, ny, weight_rows, half), b16),
            dma((2,)),
            dma((4,)),
            dma((4,)),
            dma((nx,)),
            dma((nx,)),
            dma((nz,)),
            dma((nz,)),
        ],
        compiler_params=pltpu.CompilerParams(has_side_effects=True, vmem_limit_bytes=32 << 20),
        name="front",
    )(branches, short_taps, skip_gain[None, :], long_filter, out_weight)

    scale = 1.0 / math.sqrt(float(rows * seq_size))
    convolved = pl.pallas_call(
        functools.partial(convolve_kernel, scale),
        out_shape=shape(slots, b16),
        in_specs=vmem(2),
        out_specs=vmem(1)[0],
        scratch_shapes=[
            pltpu.VMEM((SHIFTS + blocks, LANES), f32),
            pltpu.VMEM((8 + blocks, LANES), f32),
            pltpu.VMEM((blocks, SHIFTS * LANES), b16),
            pltpu.VMEM((blocks, LANES), f32),
            pltpu.VMEM((blocks, GROUP, LANES), f32),
        ],
        compiler_params=pltpu.CompilerParams(vmem_limit_bytes=32 << 20),
        name="convolve",
    )(signal, filters)

    steps = nz // 2 + 1
    chips = tp_size // 2
    return pl.pallas_call(
        back_kernel,
        out_shape=shape((rows, columns), b16),
        in_specs=vmem(5),
        out_specs=vmem(1)[0],
        scratch_shapes=[
            pltpu.VMEM(slots, b16),
            pltpu.VMEM((tp_size, rows, channels), b16),
            pltpu.VMEM((nz, nx, ny, weight_rows, half), b16),
            pltpu.VMEM((nx, nz, ny, weight_rows, half), b16),
            pltpu.VMEM((rows, half), f32),
            dma((2,)),
            dma((2, steps)),
            dma((2, steps)),
            dma((nx,)),
            dma((nx,)),
            dma((chips,)),
            dma((chips,)),
            dma((tp_size,)),
        ],
        compiler_params=pltpu.CompilerParams(has_side_effects=True, vmem_limit_bytes=32 << 20),
        name="back",
    )(convolved, gate, direct, weight_a, weight_b)


def solution(mesh):
    in_specs = (P(None, "seq", "tp"), P(None, None, "tp"), P("tp"), P("seq", "tp"), P("seq", "tp"))
    return jax.shard_map(
        functools.partial(body, mesh.shape["seq"], mesh.shape["tp"]),
        mesh=mesh,
        in_specs=in_specs,
        out_specs=P("seq", "tp"),
        check_vma=False,
    )
```

profile of v0, /device:TPU:16, one launch (start us, length us, event | category | flops | bytes accessed | tf_op | source)
XLA Modules:
  0.0 133.6 jit_solution(13146346560445514872)
XLA Ops:
  0.0 0.0 copy-start
  0.0 1.1 copy-done
  1.1 0.0 copy-start.1
  1.1 1.0 copy-done.1
  2.2 0.0 copy-start.2
  2.2 0.8 copy-done.2
  3.0 0.0 copy-start.3
  3.0 0.7 copy-done.3
  3.8 0.0 copy-start.4
  3.8 0.7 copy-done.4
  4.4 54.3 %front.1 = (f32[256,512]{1,0:T(8,128)S(1)}, f32[256,512]{1,0:T(8,128)S(1)}, f32[8,128,128]{2,1,0:T(8,128)S(1)}, f32[8,128,128]{2,1,0:T(8,128)S(1)}, bf16[4,2,64,...) custom-call(bf16[3,256,512]{2,1,0:T(8,128)(2,1)S(1)} %copy-done, f32[3,3,512]{2,1,0:T(4,128)S(1)} %copy-done.3, ...), custom_call_target="tpu_custom_call" | custom-call | tf_op jit(solution)/shard_map/front/pallas_call | solution.py:348
  58.7 12.7 %convolve.1.convolved = bf16[64,16,128]{2,1,0:T(8,128)(2,1)S(1)} custom-call(f32[8,128,128]{2,1,0:T(8,128)S(1)} %get-tuple-element.11.signal, f32[8,128,128]{2,1,0:T(8,128)S(1)} %get-tuple-element.12.long_filter), custom_call_target="tpu_custom_call" | custom-call | tf_op jit(solution)/shard_map/convolve/pallas_call | solution.py:383
  71.4 61.4 %back.1 = bf16[256,512]{1,0:T(8,128)(2,1)S(1)} custom-call(bf16[64,16,128]{2,1,0:T(8,128)(2,1)S(1)} %convolve.1.convolved, f32[256,512]{1,0:T(8,128)S(1)} %get-tuple-element.13.gate, f32[256,512]{1,0:T(8,128)S(1)} %get-tuple-element.14.direct, bf16[4,2,64,256]{3,2,1,0:T(8,128)(2,1)S(1)} %get-tuple-element.15.weight_a_in, ...), custom_call_target="tpu_custom_call" | custom-call | tf_op jit(solution)/shard_map/back/pallas_call | solution.py:401
  132.9 0.7 copy.7
Async XLA Ops:
  0.0 1.1 copy-start
  1.1 1.0 copy-start.1
  2.2 0.8 copy-start.2
  3.0 0.7 copy-start.3
  3.8 0.7 copy-start.4
where the time goes:
time: 134 us
  Pallas kernels  128 us (96%)
  local copies, waits for them, and re-layouts  5.14 us (4%)
    pallas_call x1, Pallas kernels, body(): pl.pallas_call(back_kernel, out_shape=shape((rows, columns), b16), in_spe...  61.4 us
    pallas_call x1, Pallas kernels, body(): pl.pallas_call(front_kernel, out_shape=[shape((rows, channels), f32), sha...  54.3 us
    pallas_call x1, Pallas kernels, body(): pl.pallas_call(functools.partial(convolve_kernel, scale), out_shape=shape...  12.7 us
    unnamed x11, local copies, waits for them, and re-layouts  5.14 us

commit v1 on v0

v1 whole, which is shorter than its diff:
```python
import functools
import math

import jax
import jax.numpy as jnp
from jax import lax
from jax.experimental import pallas as pl
from jax.experimental.pallas import tpu as pltpu
from jax.sharding import PartitionSpec as P

MESH = pl.DeviceIdType.MESH
LANES = 128
GROUP = 8
SHIFTS = 16


def ring_sizes(seq_size):
    return (seq_size // 8, 4, 2) if seq_size >= 32 else (seq_size // 4, 2, 2)


def place(seq_size):
    nz, nx, ny = ring_sizes(seq_size)
    me = lax.axis_index("seq")
    return me // (nx * ny), (me // ny) % nx, me % ny


def remote(src, dst, send_sem, recv_sem, device_id):
    return pltpu.make_async_remote_copy(
        src_ref=src,
        dst_ref=dst,
        send_sem=send_sem,
        recv_sem=recv_sem,
        device_id=device_id,
        device_id_type=MESH,
    )


def scatter_start(send, land, send_sem, recv_sem):
    count = send.shape[0]
    me = lax.axis_index("seq")

    def step(t, carry):
        peer = lax.rem(me + t, count)
        remote(send.at[peer], land.at[me], send_sem, recv_sem, {"seq": peer}).start()
        return carry

    lax.fori_loop(1, count, step, 0)
    land[me] = send[me]


def scatter_wait(send, land, send_sem, recv_sem):
    others = pl.ds(0, send.shape[0] - 1)
    copy = remote(send.at[others], land.at[others], send_sem, recv_sem, {"seq": 0})
    copy.wait_recv()
    return copy


def pack_rows(block_of, halves, send, column, width):
    parts = [block_of(h).T.reshape(width // GROUP, GROUP, LANES) for h in range(halves)]
    send[pl.ds(column // GROUP, width // GROUP)] = jnp.concatenate(parts, axis=1).astype(send.dtype)


def unpack_channels(land, wide, out):
    wide[...] = land[...].astype(jnp.float32).reshape(wide.shape)
    blocks = out.shape[1]
    for j in range(GROUP):
        out[j] = wide[pl.ds(j, blocks, stride=GROUP), :]


def block_kernel(
    scale, branches, taps, gain, long_filter, weight, out,
    halo, extended, send_f, send_s, land_f, land_s, land_b, wide, gate, direct, signal, filters,
    padded, filter_rows, shifted, total, first_a, first_b, weight_a, weight_b, gathered, product,
    round_sems, halo_sems, a2a_sems, y_sems, xa_send, xa_recv, zb_send, zb_recv,
    ring_send, ring_recv, xb_send, xb_recv, tp_send, tp_recv,
):
    seq_size, tp_size = land_f.shape[0], gathered.shape[0]
    nz, nx, ny = ring_sizes(seq_size)
    z, x, y = place(seq_size)
    me, mine = lax.axis_index("seq"), lax.axis_index("tp")
    rows, channels = long_filter.shape
    halves = rows // LANES
    width = min(LANES, channels)
    half_columns = first_a.shape[-1]

    def at(z, x, y):
        return {"seq": (z * nx + x) * ny + y}

    x_peers = [at(z, lax.rem(x + t, nx), y) for t in range(1, nx)]
    z_peers = [at(lax.rem(z + t, nz), x, y) for t in range(1, nz)]
    tp_peers = [{"tp": lax.rem(mine + t, tp_size)} for t in range(1, tp_size)]
    other_y = at(z, x, 1 - y)
    following = {"seq": lax.rem(me + 1, seq_size)}
    leading = {"seq": lax.rem(me + seq_size - 1, seq_size)}

    barrier = pltpu.get_barrier_semaphore()
    greeted = [other_y, following, leading] + x_peers + z_peers + tp_peers
    for peer in greeted:
        pl.semaphore_signal(barrier, inc=1, device_id=peer, device_id_type=MESH)
    first_a[x, y] = weight[:, :half_columns]
    first_b[z, y] = weight[:, half_columns:]
    for column in range(0, channels, width):
        pack_rows(
            lambda h: long_filter[h * LANES : (h + 1) * LANES, column : column + width],
            halves, send_f, column, width,
        )
    pl.semaphore_wait(barrier, len(greeted))
    for peer in x_peers:
        pl.semaphore_signal(round_sems.at[0], inc=1, device_id=peer, device_id_type=MESH)
    halo_copy = remote(
        branches.at[:, pl.ds(rows - 16, 16), :], halo, halo_sems.at[0], halo_sems.at[1], following
    )
    halo_copy.start()
    y_a = remote(first_a.at[x, y], first_a.at[x, y], y_sems.at[0], y_sems.at[1], other_y)
    y_b = remote(first_b.at[z, y], first_b.at[z, y], y_sems.at[2], y_sems.at[3], other_y)
    y_a.start()
    y_b.start()
    pl.semaphore_wait(round_sems.at[0], nx - 1)
    pl.semaphore_signal(round_sems.at[1], inc=1, device_id=other_y, device_id_type=MESH)
    pl.semaphore_wait(round_sems.at[1], 1)

    scatter_start(send_f, land_f, a2a_sems.at[0], a2a_sems.at[1])
    halo_copy.wait()
    first = me == 0
    for column in range(0, channels, width):
        span = slice(column, column + width)
        mixed = []
        for branch in range(3):
            before = halo[branch, :, span].astype(jnp.float32)
            extended[branch, 0:16, :] = jnp.where(first, 0.0, before)
            extended[branch, 16:, :] = branches[branch, :, span].astype(jnp.float32)
            mix = taps[0, branch : branch + 1, span] * extended[branch, 16 : 16 + rows, :]
            for lag in (1, 2):
                mix += taps[lag, branch : branch + 1, span] * extended[branch, 16 - lag : 16 - lag + rows, :]
            mixed.append(mix)
        made = mixed[1] * mixed[2]
        gate[:, span] = mixed[0]
        direct[:, span] = gain[0:1, span] * made
        pack_rows(lambda h: made[h * LANES : (h + 1) * LANES], halves, send_s, column, width)
    scatter_start(send_s, land_s, a2a_sems.at[2], a2a_sems.at[3])
    y_a.wait()
    y_b.wait()
    copy_f = scatter_wait(send_f, land_f, a2a_sems.at[0], a2a_sems.at[1])
    unpack_channels(land_f, wide, filters)
    copy_s = scatter_wait(send_s, land_s, a2a_sems.at[2], a2a_sems.at[3])

    sent = [copy_f]
    for t, peer in enumerate(x_peers):
        sent.append(remote(first_a.at[x], first_a.at[x], xa_send.at[t], xa_recv.at[x], peer))
    for t, peer in enumerate(z_peers):
        sent.append(remote(first_b.at[z], first_b.at[z], zb_send.at[t], zb_recv.at[z], peer))
    for copy in sent[1:]:
        copy.start()
    unpack_channels(land_s, wide, signal)

    ring_peers = at(lax.rem(z + 1, nz), x, y), at(lax.rem(z + nz - 1, nz), x, y)
    middle = nx // 2

    def ring_copy(way, t):
        block = lax.rem(z + nz - (t - 1), nz) if way == 0 else lax.rem(z + (t - 1), nz)
        piece = weight_a.at[block]
        if 2 * t == nz:
            piece = weight_a.at[block, pl.ds(way * middle, middle)]
        return remote(piece, piece, ring_send.at[way, t], ring_recv.at[way, t], ring_peers[way])

    def ring_start(t):
        for way in range(2):
            ring_copy(way, t).start()

    def ring_wait(t):
        for way in range(2):
            ring_copy(way, t).wait_recv()

    def first_ring():
        for t in range(1, nx):
            source = lax.rem(x + nx - t, nx)
            remote(first_a.at[source], first_a.at[source], xa_send.at[t], xa_recv.at[source], other_y).wait_recv()
        weight_a[z] = first_a[...]
        ring_start(1)

    convolve(scale, signal, filters, padded, filter_rows, shifted, total, wide, first_ring)
    copy_s.wait_send()
    send_s[...] = wide[...].reshape(send_s.shape).astype(send_s.dtype)
    scatter_start(send_s, land_b, a2a_sems.at[4], a2a_sems.at[5])
    for t in range(1, nz):
        source = lax.rem(z + nz - t, nz)
        remote(first_b.at[source], first_b.at[source], zb_send.at[0], zb_recv.at[source], other_y).wait_recv()
    weight_b[x] = first_b[...]
    for t, peer in enumerate(x_peers):
        copy = remote(weight_b.at[x], weight_b.at[x], xb_send.at[t], xb_recv.at[x], peer)
        copy.start()
        sent.append(copy)
    ring_wait(1)
    if nz // 2 >= 2:
        ring_start(2)
    sent.append(scatter_wait(send_s, land_b, a2a_sems.at[4], a2a_sems.at[5]))

    for column in range(0, channels, width):
        slots = pl.ds(column // GROUP, width // GROUP)
        arrived = land_b[slots].astype(jnp.float32)
        for h in range(halves):
            block = arrived[:, h * GROUP : (h + 1) * GROUP, :].reshape(width, LANES).T
            span = (slice(h * LANES, (h + 1) * LANES), slice(column, column + width))
            gated = gate[span] * (block + direct[span])
            gathered[mine, h * LANES : (h + 1) * LANES, column : column + width] = gated.astype(gathered.dtype)
    chips = tp_size // 2
    chip, core = mine // 2, lax.rem(mine, 2)

    def tp_copy(slot, kind, to):
        return remote(gathered.at[slot], gathered.at[slot], tp_send.at[kind, slot], tp_recv.at[slot], {"tp": to})

    def up(slot):
        return tp_copy(slot, 0, mine + 2)

    def down(slot):
        return tp_copy(slot, 1, mine - 2)

    def side(slot):
        return tp_copy(slot, 2, mine + 1 - 2 * core)

    pl.when(chip < chips - 1)(lambda: up(mine).start())
    pl.when(chip > 0)(lambda: down(mine).start())
    side(mine).start()
    for t in range(1, chips):
        if t + 2 <= nz // 2:
            ring_wait(t + 1)
            ring_start(t + 2)

        @pl.when(chip >= t)
        def _():
            slot = mine - 2 * t
            side(slot).wait_recv()
            pl.when(chip < chips - 1)(lambda: up(slot).start())
            side(slot).start()

        @pl.when(chip + t < chips)
        def _():
            slot = mine + 2 * t
            side(slot).wait_recv()
            pl.when(chip > 0)(lambda: down(slot).start())
            side(slot).start()

    for k in range(chips):
        side(2 * k + 1 - core).wait_recv()
    if nz // 2 >= 2:
        ring_wait(nz // 2)
    for t in range(1, nx):
        source = lax.rem(x + nx - t, nx)
        remote(weight_b.at[source], weight_b.at[source], xb_send.at[0], xb_recv.at[source], other_y).wait_recv()

    for part in range(2):
        product[...] = jnp.zeros_like(product)

        def add(block, carry):
            tile = weight_a[block] if part == 0 else weight_b[:, block]
            product[...] += jnp.dot(
                gathered[block], tile.reshape(channels, half_columns), preferred_element_type=jnp.float32
            )
            return carry

        lax.fori_loop(0, tp_size, add, 0)
        out[:, part * half_columns : (part + 1) * half_columns] = product[...].astype(out.dtype)

    for copy in sent:
        copy.wait_send()
    for t in range(1, nz // 2 + 1):
        for way in range(2):
            ring_copy(way, t).wait_send()
    for k in range(chips):
        slot = 2 * k + core
        side(slot).wait_send()
        pl.when((k <= chip) & (chip < chips - 1))(lambda: up(slot).wait_send())
        pl.when((k >= chip) & (chip > 0))(lambda: down(slot).wait_send())


def convolve(scale, signal, long_filter, padded, taps, shifted, total, wide, midway):
    blocks = signal.shape[1]
    step = min(2 * SHIFTS, blocks)
    padded[0:SHIFTS, :] = jnp.zeros((SHIFTS, LANES), jnp.float32)
    taps[0:8, :] = jnp.zeros((8, LANES), jnp.float32)
    row = lax.broadcasted_iota(jnp.int32, (LANES, LANES), 0)
    lane = lax.broadcasted_iota(jnp.int32, (LANES, LANES), 1)
    causal = lane >= row

    def rolled(block):
        line = jnp.broadcast_to(taps[8 + block : 9 + block, :], (LANES, LANES))
        return pltpu.roll(line, 0, 1, stride=1, stride_axis=0)

    def channel(j, carry):
        pl.when(j == GROUP // 2)(midway)
        padded[SHIFTS:, :] = signal[j]
        taps[8:, :] = long_filter[j]
        for shift in range(SHIFTS):
            shifted[:, shift * LANES : (shift + 1) * LANES] = padded[
                SHIFTS - shift : SHIFTS - shift + blocks, :
            ].astype(jnp.bfloat16)
        for start in range(0, blocks, step):
            height = blocks - start
            spans = range(start, min(start + step, blocks), SHIFTS)
            last = [rolled(span - 1) for span in spans]
            partial = None
            for shift in range(0, SHIFTS, 2):
                tiles = []
                for extra in range(2):
                    here = [rolled(span + shift + extra) for span in spans]
                    tiles.append(
                        jnp.concatenate(
                            [jnp.where(causal, h, b).astype(jnp.bfloat16) for h, b in zip(here, last)], axis=1
                        )
                    )
                    last = here
                term = jnp.dot(
                    shifted[0:height, shift * LANES : (shift + 2) * LANES],
                    jnp.concatenate(tiles, axis=0),
                    preferred_element_type=jnp.float32,
                )
                partial = term if partial is None else partial + term
            if start == 0:
                total[...] = partial[:, :LANES]
            else:
                total[start:, :] += partial[:, :LANES]
            if len(spans) > 1:
                total[start + SHIFTS :, :] += partial[: height - SHIFTS, LANES:]
        wide[pl.ds(j, blocks, stride=GROUP), :] = total[...] * scale
        return carry

    lax.fori_loop(0, GROUP, channel, 0)


def body(seq_size, tp_size, branches, short_taps, skip_gain, long_filter, out_weight):
    rows, channels = long_filter.shape
    weight_rows, columns = out_weight.shape
    nz, nx, ny = ring_sizes(seq_size)
    assert channels == GROUP * seq_size and nz == tp_size and nx * ny * weight_rows == channels
    halves = rows // LANES
    blocks = halves * seq_size
    half = columns // 2
    slots = (seq_size, halves * GROUP, LANES)
    f32, b16 = jnp.float32, jnp.bfloat16
    dma = pltpu.SemaphoreType.DMA
    steps = nz // 2 + 1
    scale = 1.0 / math.sqrt(float(rows * seq_size))
    return pl.pallas_call(
        functools.partial(block_kernel, scale),
        out_shape=jax.ShapeDtypeStruct((rows, columns), b16),
        in_specs=[pl.BlockSpec(memory_space=pltpu.VMEM)] * 5,
        out_specs=pl.BlockSpec(memory_space=pltpu.VMEM),
        scratch_shapes=[
            pltpu.VMEM((3, 16, channels), b16),
            pltpu.VMEM((3, 16 + rows, min(LANES, channels)), f32),
            *[pltpu.VMEM(slots, b16)] * 5,
            pltpu.VMEM((blocks * GROUP, LANES), f32),
            *[pltpu.VMEM((rows, channels), f32)] * 2,
            *[pltpu.VMEM((GROUP, blocks, LANES), f32)] * 2,
            pltpu.VMEM((SHIFTS + blocks, LANES), f32),
            pltpu.VMEM((8 + blocks, LANES), f32),
            pltpu.VMEM((blocks, SHIFTS * LANES), b16),
            pltpu.VMEM((blocks, LANES), f32),
            pltpu.VMEM((nx, ny, weight_rows, half), b16),
            pltpu.VMEM((nz, ny, weight_rows, half), b16),
            pltpu.VMEM((nz, nx, ny, weight_rows, half), b16),
            pltpu.VMEM((nx, nz, ny, weight_rows, half), b16),
            pltpu.VMEM((tp_size, rows, channels), b16),
            pltpu.VMEM((rows, half), f32),
            pltpu.SemaphoreType.REGULAR((2,)),
            dma((2,)),
            dma((6,)),
            dma((4,)),
            dma((nx,)),
            dma((nx,)),
            dma((nz,)),
            dma((nz,)),
            dma((2, steps)),
            dma((2, steps)),
            dma((nx,)),
            dma((nx,)),
            dma((3, tp_size)),
            dma((tp_size,)),
        ],
        compiler_params=pltpu.CompilerParams(has_side_effects=True, collective_id=0, vmem_limit_bytes=40 << 20),
        name="hyena",
    )(branches, short_taps, skip_gain[None, :], long_filter, out_weight)


def solution(mesh):
    in_specs = (P(None, "seq", "tp"), P(None, None, "tp"), P("tp"), P("seq", "tp"), P("seq", "tp"))
    return jax.shard_map(
        functools.partial(body, mesh.shape["seq"], mesh.shape["tp"]),
        mesh=mesh,
        in_specs=in_specs,
        out_specs=P("seq", "tp"),
        check_vma=False,
    )
```

time: 134 us -> 96.9 us (0.72)
  the two profiles are of different devices: /device:TPU:16 before, /device:TPU:1 now
where the time goes in v1:
time: 96.9 us; the launch traced here: 96.5 us
  Pallas kernels  91.4 us (94%)
  local copies, waits for them, and re-layouts  5.14 us (5%)
    pallas_call x1, Pallas kernels, body(): pl.pallas_call(functools.partial(block_kernel, scale), out_shape=jax.Shap...  91.4 us
    unnamed x11, local copies, waits for them, and re-layouts  5.14 us

profile of v1, /device:TPU:1, one launch (start us, length us, event | category | flops | bytes accessed | tf_op | source)
XLA Modules:
  0.0 96.5 jit_solution(10377110954953289102)
XLA Ops:
  0.0 0.0 copy-start
  0.0 1.1 %copy-done = bf16[3,256,512]{2,1,0:T(8,128)(2,1)S(1)} copy-done((bf16[3,256,512]{2,1,0:T(8,128)(2,1)S(1)}, bf16[3,256,512]{2,1,0:T(8,128)(2,1)}, u32[]{:S(2)}) %copy-start) | copy-done | bytes 786456
  1.1 0.0 copy-start.1
  1.1 1.0 %copy-done.1 = f32[256,512]{1,0:T(8,128)S(1)} copy-done((f32[256,512]{1,0:T(8,128)S(1)}, f32[256,512]{1,0:T(8,128)}, u32[]{:S(2)}) %copy-start.1) | copy-done | bytes 524312
  2.2 0.0 copy-start.2
  2.2 0.8 copy-done.2
  3.0 0.0 copy-start.3
  3.0 0.7 copy-done.3
  3.8 0.0 copy-start.4
  3.8 0.7 copy-done.4
  4.4 91.4 %hyena.1 = bf16[256,512]{1,0:T(8,128)(2,1)S(1)} custom-call(bf16[3,256,512]{2,1,0:T(8,128)(2,1)S(1)} %copy-done, f32[3,3,512]{2,1,0:T(4,128)S(1)} %copy-done.3, f32[1,512]{1,0:T(1,128)S(1)} %bitcast.1, f32[256,512]{1,0:T(8,128)S(1)} %copy-done.1, bf16[64,512]{1,0:T(8,128)(2,1)S(1)} %copy-done.2), custom_call_target="tpu_custom_call" | custom-call | tf_op jit(solution)/shard_map/hyena/pallas_call | solution.py:343
  95.8 0.7 copy.7
Async XLA Ops:
  0.0 1.1 %copy-start = (bf16[3,256,512]{2,1,0:T(8,128)(2,1)S(1)}, bf16[3,256,512]{2,1,0:T(8,128)(2,1)}, u32[]{:S(2)}) copy-start(bf16[3,256,512]{2,1,0:T(8,128)(2,1)} %branches.1) | copy-start | bytes 2359300
  1.1 1.0 %copy-start.1 = (f32[256,512]{1,0:T(8,128)S(1)}, f32[256,512]{1,0:T(8,128)}, u32[]{:S(2)}) copy-start(f32[256,512]{1,0:T(8,128)} %long_filter.1) | copy-start | bytes 1572868
  2.2 0.8 copy-start.2
  3.0 0.7 copy-start.3
  3.8 0.7 copy-start.4

commit v2 on v1

v2 whole, which is shorter than its diff:
```python
import functools
import math

import jax
import jax.numpy as jnp
from jax import lax
from jax.experimental import pallas as pl
from jax.experimental.pallas import tpu as pltpu
from jax.sharding import PartitionSpec as P

MESH = pl.DeviceIdType.MESH
LANES = 128
GROUP = 8
SHIFTS = 16
SCHEDULE = {
    "halo": ("y", "as"),
    "sent": ("b1",),
    "filter": ("b2",),
    "signal": ("b3", "n0", "n1", "a1"),
    1: ("b4", "n2"),
    3: ("b5", "n3", "n4", "a2"),
    5: ("a3",),
    "gated": ("bl", "a4"),
    "passed 3": ("a5", "bd"),
}


def ring_sizes(seq_size):
    return (seq_size // 8, 4, 2) if seq_size >= 32 else (seq_size // 4, 2, 2)


def place(seq_size):
    nz, nx, ny = ring_sizes(seq_size)
    me = lax.axis_index("seq")
    return me // (nx * ny), (me // ny) % nx, me % ny


def remote(src, dst, send_sem, recv_sem, device_id):
    return pltpu.make_async_remote_copy(
        src_ref=src,
        dst_ref=dst,
        send_sem=send_sem,
        recv_sem=recv_sem,
        device_id=device_id,
        device_id_type=MESH,
    )


def scatter_start(send, land, send_sem, recv_sem):
    count = send.shape[0]
    me = lax.axis_index("seq")

    def step(t, carry):
        peer = lax.rem(me + t, count)
        remote(send.at[peer], land.at[me], send_sem, recv_sem, {"seq": peer}).start()
        return carry

    lax.fori_loop(1, count, step, 0)
    land[me] = send[me]


def scatter_wait(send, land, send_sem, recv_sem):
    others = pl.ds(0, send.shape[0] - 1)
    copy = remote(send.at[others], land.at[others], send_sem, recv_sem, {"seq": 0})
    copy.wait_recv()
    return copy


def pack_rows(block_of, halves, send, column, width):
    parts = [block_of(h).T.reshape(width // GROUP, GROUP, LANES) for h in range(halves)]
    send[pl.ds(column // GROUP, width // GROUP)] = jnp.concatenate(parts, axis=1).astype(send.dtype)


def unpack_channels(land, wide, out):
    wide[...] = land[...].astype(jnp.float32).reshape(wide.shape)
    blocks = out.shape[1]
    for j in range(GROUP):
        out[j] = wide[pl.ds(j, blocks, stride=GROUP), :]


def block_kernel(
    scale, branches, taps, gain, long_filter, weight, out,
    halo, extended, send_f, send_s, land_f, land_s, land_b, wide, gate, direct, signal, filters,
    padded, filter_rows, shifted, total, weight_a, weight_b, gathered, product,
    round_sems, halo_sems, a2a_sems, y_sems, xa_send, xa_recv, za_send, za_recv, zb_send, zb_recv,
    xb_send, xb_recv, far_send, far_recv, back_recv, tp_send, tp_recv,
):
    seq_size, tp_size = land_f.shape[0], gathered.shape[0]
    nz, nx, ny = ring_sizes(seq_size)
    z, x, y = place(seq_size)
    me, mine = lax.axis_index("seq"), lax.axis_index("tp")
    rows, channels = long_filter.shape
    halves = rows // LANES
    width = min(LANES, channels)
    columns_a = weight_a.shape[-1]

    def at(z, x, y):
        return {"seq": (z * nx + x) * ny + y}

    x_peers = [at(z, lax.rem(x + t, nx), y) for t in range(1, nx)]
    z_peers = [at(lax.rem(z + t, nz), x, y) for t in range(1, nz)]
    tp_peers = [{"tp": lax.rem(mine + t, tp_size)} for t in range(1, tp_size)]
    other_y = at(z, x, 1 - y)
    following = {"seq": lax.rem(me + 1, seq_size)}
    leading = {"seq": lax.rem(me + seq_size - 1, seq_size)}

    barrier = pltpu.get_barrier_semaphore()
    greeted = [other_y, following, leading] + x_peers + z_peers + tp_peers
    for peer in greeted:
        pl.semaphore_signal(barrier, inc=1, device_id=peer, device_id_type=MESH)
    weight_a[z, x, y] = weight[:, :columns_a]
    weight_b[x, z, y] = weight[:, columns_a:]
    for column in range(0, channels, width):
        pack_rows(
            lambda h: long_filter[h * LANES : (h + 1) * LANES, column : column + width],
            halves, send_f, column, width,
        )
    pl.semaphore_wait(barrier, len(greeted))
    for peer in x_peers:
        pl.semaphore_signal(round_sems.at[0], inc=1, device_id=peer, device_id_type=MESH)
    halo_copy = remote(
        branches.at[:, pl.ds(rows - 16, 16), :], halo, halo_sems.at[0], halo_sems.at[1], following
    )
    halo_copy.start()
    y_a = remote(weight_a.at[z, x, y], weight_a.at[z, x, y], y_sems.at[0], y_sems.at[1], other_y)
    y_b = remote(weight_b.at[x, z, y], weight_b.at[x, z, y], y_sems.at[2], y_sems.at[3], other_y)
    y_a.start()
    y_b.start()
    pl.semaphore_wait(round_sems.at[0], nx - 1)
    pl.semaphore_signal(round_sems.at[1], inc=1, device_id=other_y, device_id_type=MESH)
    pl.semaphore_wait(round_sems.at[1], 1)

    sent = []
    z_pair = at(lax.rem(z + 1, nz), x, y), at(lax.rem(z + nz - 1, nz), x, y)
    x_pair = at(z, lax.rem(x + 1, nx), y), at(z, lax.rem(x + nx - 1, nx), y)

    def z_block(way, t):
        return lax.rem(z + nz - t, nz) if way == 0 else lax.rem(z + t, nz)

    def a_ring(way, t):
        block = z_block(way, t - 1)
        piece = weight_a.at[block, pl.ds(way * (nx // 2), nx // 2)] if 2 * t == nz else weight_a.at[block]
        return remote(piece, piece, za_send.at[way, t], za_recv.at[way, t], z_pair[way])

    def b_ring(way, t):
        block = z_block(way, t - 1)
        piece = weight_b.at[x, block, way] if 2 * t == nz else weight_b.at[x, block]
        return remote(piece, piece, zb_send.at[way, t], zb_recv.at[way, t], z_pair[way])

    def b_next(way, block):
        piece = weight_b.at[x, block]
        return remote(piece, piece, xb_send.at[way, block], xb_recv.at[way, block], x_pair[way])

    def b_far(way):
        source = lax.rem(x + nx - 1, nx) if way == 0 else lax.rem(x + 1, nx)
        piece = weight_b.at[source, pl.ds(way * (nz // 2), nz // 2)]
        return remote(piece, piece, far_send.at[way], far_recv.at[way], x_pair[way])

    def y_done():
        y_a.wait()
        y_b.wait()

    def a_spread():
        for t, peer in enumerate(x_peers):
            copy = remote(weight_a.at[z, x], weight_a.at[z, x], xa_send.at[t], xa_recv.at[x], peer)
            copy.start()
            sent.append(copy)

    def a_step(t):
        if t == 1:
            for i in range(1, nx):
                source = lax.rem(x + nx - i, nx)
                arrived = weight_a.at[z, source]
                remote(arrived, arrived, xa_send.at[0], xa_recv.at[source], other_y).wait_recv()
        for way in range(2):
            if t > 1:
                a_ring(way, t - 1).wait_recv()
        for way in range(2):
            if 2 * t <= nz:
                a_ring(way, t).start()

    def b_step(t):
        for way in range(2):
            if t > 1:
                b_ring(way, t - 1).wait_recv()
        for way in range(2):
            if 2 * t <= nz:
                b_ring(way, t).start()

    def b_along(t):
        for block in [z_block(0, t)] if t == 0 or 2 * t == nz else [z_block(0, t), z_block(1, t)]:
            for way in range(2):
                b_next(way, block).start()

    def b_last():
        for way in range(2):
            for block in range(nz):
                b_next(way, block).wait_recv()
        for way in range(2):
            b_far(way).start()

    def b_done():
        for way in range(2):
            b_far(way).wait_recv()

    steps = {"y": y_done, "as": a_spread, "bl": b_last, "bd": b_done}
    for t in range(1, nz // 2 + 2):
        steps[f"a{t}"] = functools.partial(a_step, t)
        steps[f"b{t}"] = functools.partial(b_step, t)
        steps[f"n{t - 1}"] = functools.partial(b_along, t - 1)

    def weight_steps(point):
        for name in SCHEDULE.get(point, ()):
            steps[name]()

    def pump(j):
        for channel in range(GROUP):
            if channel in SCHEDULE:
                pl.when(j == channel)(functools.partial(weight_steps, channel))

    scatter_start(send_f, land_f, a2a_sems.at[0], a2a_sems.at[1])
    halo_copy.wait()
    weight_steps("halo")
    first = me == 0
    for column in range(0, channels, width):
        span = slice(column, column + width)
        mixed = []
        for branch in range(3):
            before = halo[branch, :, span].astype(jnp.float32)
            extended[branch, 0:16, :] = jnp.where(first, 0.0, before)
            extended[branch, 16:, :] = branches[branch, :, span].astype(jnp.float32)
            mix = taps[0, branch : branch + 1, span] * extended[branch, 16 : 16 + rows, :]
            for lag in (1, 2):
                mix += taps[lag, branch : branch + 1, span] * extended[branch, 16 - lag : 16 - lag + rows, :]
            mixed.append(mix)
        made = mixed[1] * mixed[2]
        gate[:, span] = mixed[0]
        direct[:, span] = gain[0:1, span] * made
        pack_rows(lambda h: made[h * LANES : (h + 1) * LANES], halves, send_s, column, width)
    scatter_start(send_s, land_s, a2a_sems.at[2], a2a_sems.at[3])
    weight_steps("sent")
    copy_f = scatter_wait(send_f, land_f, a2a_sems.at[0], a2a_sems.at[1])
    sent.append(copy_f)
    unpack_channels(land_f, wide, filters)
    weight_steps("filter")
    copy_s = scatter_wait(send_s, land_s, a2a_sems.at[2], a2a_sems.at[3])
    unpack_channels(land_s, wide, signal)
    weight_steps("signal")
    convolve(scale, signal, filters, padded, filter_rows, shifted, total, wide, pump)
    copy_s.wait_send()
    send_s[...] = wide[...].reshape(send_s.shape).astype(send_s.dtype)
    parts = tp_send.shape[2]
    per_part = seq_size // parts
    my_part = me // per_part

    def part_at(k):
        return lax.rem(my_part + parts - k, parts)

    for k in range(parts):

        def send_back(i, carry):
            peer = lax.rem(my_part + k, parts) * per_part + lax.rem(me + i, per_part)
            remote(send_s.at[peer], land_b.at[me], a2a_sems.at[4], back_recv.at[my_part], {"seq": peer}).start()
            return carry

        lax.fori_loop(1 if k == 0 else 0, per_part, send_back, 0)
    land_b[me] = send_s[me]
    sent.append(remote(send_s.at[pl.ds(1, seq_size - 1)], land_b.at[pl.ds(1, seq_size - 1)], a2a_sems.at[4], a2a_sems.at[5], other_y))
    weight_steps("back")

    chips = tp_size // 2
    chip, core = mine // 2, lax.rem(mine, 2)

    def tp_copy(slot, k, kind, to):
        piece = gathered.at[slot, :, pl.ds(pl.multiple_of(part_at(k) * width, width), width)]
        return remote(piece, piece, tp_send.at[kind, slot, k], tp_recv.at[slot, k], {"tp": to})

    def up(slot, k):
        return tp_copy(slot, k, 0, mine + 2)

    def down(slot, k):
        return tp_copy(slot, k, 1, mine - 2)

    def side(slot, k):
        return tp_copy(slot, k, 2, mine + 1 - 2 * core)

    for k in range(parts):
        part = part_at(k)
        landed = land_b.at[pl.ds(part * per_part, per_part - 1 if k == 0 else per_part)]
        remote(landed, landed, a2a_sems.at[4], back_recv.at[part], other_y).wait_recv()
        arrived = land_b[pl.ds(part * per_part, per_part)].astype(jnp.float32)
        columns = pl.ds(pl.multiple_of(part * width, width), width)
        for h in range(halves):
            block = arrived[:, h * GROUP : (h + 1) * GROUP, :].reshape(width, LANES).T
            span = (pl.ds(h * LANES, LANES), columns)
            gathered[mine, h * LANES : (h + 1) * LANES, columns] = (
                gate[span] * (block + direct[span])
            ).astype(gathered.dtype)
        pl.when(chip < chips - 1)(lambda: up(mine, k).start())
        pl.when(chip > 0)(lambda: down(mine, k).start())
        side(mine, k).start()
    weight_steps("gated")

    def pass_on(t):
        for k in range(parts):

            @pl.when(chip >= t)
            def _():
                slot = mine - 2 * t
                side(slot, k).wait_recv()
                pl.when(chip < chips - 1)(lambda: up(slot, k).start())
                side(slot, k).start()

            @pl.when(chip + t < chips)
            def _():
                slot = mine + 2 * t
                side(slot, k).wait_recv()
                pl.when(chip > 0)(lambda: down(slot, k).start())
                side(slot, k).start()

    def add(slot):
        for tile, span in (
            (weight_a[slot], slice(0, columns_a)),
            (weight_b[:, slot], slice(columns_a, columns_a + weight_b.shape[-1])),
        ):
            product[:, span] += jnp.dot(
                gathered[slot], tile.reshape(channels, tile.shape[-1]), preferred_element_type=jnp.float32
            )

    def add_pair(slot):
        other = slot + 1 - 2 * core
        for k in range(parts):
            side(other, k).wait_recv()
        add(slot)
        add(other)

    def add_all(t):
        pl.when(chip >= t)(lambda: add_pair(mine - 2 * t))
        if t > 0:
            pl.when(chip + t < chips)(lambda: add_pair(mine + 2 * t))

    product[...] = jnp.zeros_like(product)
    for t in range(1, chips):
        pass_on(t)
        weight_steps(f"passed {t}")
    for t in range(chips):
        add_all(t)
    out[...] = product[...].astype(out.dtype)

    for copy in sent:
        copy.wait_send()
    for way in range(2):
        for t in range(1, nz // 2 + 1):
            a_ring(way, t).wait_send()
            b_ring(way, t).wait_send()
        for block in range(nz):
            b_next(way, block).wait_send()
        b_far(way).wait_send()
    for i in range(chips):
        slot = 2 * i + core
        for k in range(parts):
            side(slot, k).wait_send()
            pl.when((i <= chip) & (chip < chips - 1))(lambda: up(slot, k).wait_send())
            pl.when((i >= chip) & (chip > 0))(lambda: down(slot, k).wait_send())


def convolve(scale, signal, long_filter, padded, taps, shifted, total, wide, midway):
    blocks = signal.shape[1]
    step = min(2 * SHIFTS, blocks)
    padded[0:SHIFTS, :] = jnp.zeros((SHIFTS, LANES), jnp.float32)
    taps[0:8, :] = jnp.zeros((8, LANES), jnp.float32)
    row = lax.broadcasted_iota(jnp.int32, (LANES, LANES), 0)
    lane = lax.broadcasted_iota(jnp.int32, (LANES, LANES), 1)
    causal = lane >= row

    def rolled(block):
        line = jnp.broadcast_to(taps[8 + block : 9 + block, :], (LANES, LANES))
        return pltpu.roll(line, 0, 1, stride=1, stride_axis=0)

    def channel(j, carry):
        midway(j)
        padded[SHIFTS:, :] = signal[j]
        taps[8:, :] = long_filter[j]
        for shift in range(SHIFTS):
            shifted[:, shift * LANES : (shift + 1) * LANES] = padded[
                SHIFTS - shift : SHIFTS - shift + blocks, :
            ].astype(jnp.bfloat16)
        for start in range(0, blocks, step):
            height = blocks - start
            spans = range(start, min(start + step, blocks), SHIFTS)
            last = [rolled(span - 1) for span in spans]
            partial = None
            for shift in range(0, SHIFTS, 2):
                tiles = []
                for extra in range(2):
                    here = [rolled(span + shift + extra) for span in spans]
                    tiles.append(
                        jnp.concatenate(
                            [jnp.where(causal, h, b).astype(jnp.bfloat16) for h, b in zip(here, last)], axis=1
                        )
                    )
                    last = here
                term = jnp.dot(
                    shifted[0:height, shift * LANES : (shift + 2) * LANES],
                    jnp.concatenate(tiles, axis=0),
                    preferred_element_type=jnp.float32,
                )
                partial = term if partial is None else partial + term
            if start == 0:
                total[...] = partial[:, :LANES]
            else:
                total[start:, :] += partial[:, :LANES]
            if len(spans) > 1:
                total[start + SHIFTS :, :] += partial[: height - SHIFTS, LANES:]
        wide[pl.ds(j, blocks, stride=GROUP), :] = total[...] * scale
        return carry

    lax.fori_loop(0, GROUP, channel, 0)


def body(seq_size, tp_size, branches, short_taps, skip_gain, long_filter, out_weight):
    rows, channels = long_filter.shape
    weight_rows, columns = out_weight.shape
    nz, nx, ny = ring_sizes(seq_size)
    assert channels == GROUP * seq_size and nz == tp_size and nx * ny * weight_rows == channels
    halves = rows // LANES
    blocks = halves * seq_size
    columns_a = columns // 4
    slots = (seq_size, halves * GROUP, LANES)
    f32, b16 = jnp.float32, jnp.bfloat16
    dma = pltpu.SemaphoreType.DMA
    steps = nz // 2 + 1
    parts = channels // min(LANES, channels)
    scale = 1.0 / math.sqrt(float(rows * seq_size))
    return pl.pallas_call(
        functools.partial(block_kernel, scale),
        out_shape=jax.ShapeDtypeStruct((rows, columns), b16),
        in_specs=[pl.BlockSpec(memory_space=pltpu.VMEM)] * 5,
        out_specs=pl.BlockSpec(memory_space=pltpu.VMEM),
        scratch_shapes=[
            pltpu.VMEM((3, 16, channels), b16),
            pltpu.VMEM((3, 16 + rows, min(LANES, channels)), f32),
            *[pltpu.VMEM(slots, b16)] * 5,
            pltpu.VMEM((blocks * GROUP, LANES), f32),
            *[pltpu.VMEM((rows, channels), f32)] * 2,
            *[pltpu.VMEM((GROUP, blocks, LANES), f32)] * 2,
            pltpu.VMEM((SHIFTS + blocks, LANES), f32),
            pltpu.VMEM((8 + blocks, LANES), f32),
            pltpu.VMEM((blocks, SHIFTS * LANES), b16),
            pltpu.VMEM((blocks, LANES), f32),
            pltpu.VMEM((nz, nx, ny, weight_rows, columns_a), b16),
            pltpu.VMEM((nx, nz, ny, weight_rows, columns - columns_a), b16),
            pltpu.VMEM((tp_size, rows, channels), b16),
            pltpu.VMEM((rows, columns), f32),
            pltpu.SemaphoreType.REGULAR((2,)),
            dma((2,)),
            dma((6,)),
            dma((4,)),
            dma((nx,)),
            dma((nx,)),
            *[dma((2, steps))] * 4,
            *[dma((2, nz))] * 2,
            *[dma((2,))] * 2,
            dma((parts,)),
            dma((3, tp_size, parts)),
            dma((tp_size, parts)),
        ],
        compiler_params=pltpu.CompilerParams(has_side_effects=True, collective_id=0, vmem_limit_bytes=40 << 20),
        name="hyena",
    )(branches, short_taps, skip_gain[None, :], long_filter, out_weight)


def solution(mesh):
    in_specs = (P(None, "seq", "tp"), P(None, None, "tp"), P("tp"), P("seq", "tp"), P("seq", "tp"))
    return jax.shard_map(
        functools.partial(body, mesh.shape["seq"], mesh.shape["tp"]),
        mesh=mesh,
        in_specs=in_specs,
        out_specs=P("seq", "tp"),
        check_vma=False,
    )
```

time: 96.9 us -> 91.5 us (0.944)
  Pallas kernels: 91.4 us -> 86 us
    pallas_call x1, Pallas kernels: 91.4 us -> 86 us  [body(): pl.pallas_call(functools.partial(block_kernel, scale), out_shape=jax.Shap...]
where the time goes in v2:
time: 91.5 us; the launch traced here: 91.1 us
  Pallas kernels  86 us (94%)
  local copies, waits for them, and re-layouts  5.14 us (6%)
    pallas_call x1, Pallas kernels, body(): pl.pallas_call(functools.partial(block_kernel, scale), out_shape=jax.Shap...  86 us
    unnamed x11, local copies, waits for them, and re-layouts  5.14 us

profile of v2, /device:TPU:1, one launch (start us, length us, event | category | flops | bytes accessed | tf_op | source)
XLA Modules:
  0.0 91.1 jit_solution(8857537250740711233)
XLA Ops:
  0.0 0.0 copy-start
  0.0 1.1 %copy-done = bf16[3,256,512]{2,1,0:T(8,128)(2,1)S(1)} copy-done((bf16[3,256,512]{2,1,0:T(8,128)(2,1)S(1)}, bf16[3,256,512]{2,1,0:T(8,128)(2,1)}, u32[]{:S(2)}) %copy-start) | copy-done | bytes 786456
  1.1 0.0 copy-start.1
  1.1 1.0 %copy-done.1 = f32[256,512]{1,0:T(8,128)S(1)} copy-done((f32[256,512]{1,0:T(8,128)S(1)}, f32[256,512]{1,0:T(8,128)}, u32[]{:S(2)}) %copy-start.1) | copy-done | bytes 524312
  2.2 0.0 copy-start.2
  2.2 0.8 copy-done.2
  3.0 0.0 copy-start.3
  3.0 0.7 copy-done.3
  3.8 0.0 copy-start.4
  3.8 0.7 copy-done.4
  4.4 86.0 %hyena.1 = bf16[256,512]{1,0:T(8,128)(2,1)S(1)} custom-call(bf16[3,256,512]{2,1,0:T(8,128)(2,1)S(1)} %copy-done, f32[3,3,512]{2,1,0:T(4,128)S(1)} %copy-done.3, f32[1,512]{1,0:T(1,128)S(1)} %bitcast.1, f32[256,512]{1,0:T(8,128)S(1)} %copy-done.1, bf16[64,512]{1,0:T(8,128)(2,1)S(1)} %copy-done.2), custom_call_target="tpu_custom_call" | custom-call | tf_op jit(solution)/shard_map/hyena/pallas_call | solution.py:435
  90.4 0.7 copy.7
Async XLA Ops:
  0.0 1.1 %copy-start = (bf16[3,256,512]{2,1,0:T(8,128)(2,1)S(1)}, bf16[3,256,512]{2,1,0:T(8,128)(2,1)}, u32[]{:S(2)}) copy-start(bf16[3,256,512]{2,1,0:T(8,128)(2,1)} %branches.1) | copy-start | bytes 2359300
  1.1 1.0 %copy-start.1 = (f32[256,512]{1,0:T(8,128)S(1)}, f32[256,512]{1,0:T(8,128)}, u32[]{:S(2)}) copy-start(f32[256,512]{1,0:T(8,128)} %long_filter.1) | copy-start | bytes 1572868
  2.2 0.8 copy-start.2
  3.0 0.7 copy-start.3
  3.8 0.7 copy-start.4

commit v3 on v2

--- a/solution.py
+++ b/solution.py
@@ -11,17 +11,20 @@
 MESH = pl.DeviceIdType.MESH
 LANES = 128
 GROUP = 8
-SHIFTS = 16
+REACH = 32
+TURN = 16
+PART_A = 2
 SCHEDULE = {
-    "halo": ("y", "as"),
-    "sent": ("b1",),
-    "filter": ("b2",),
-    "signal": ("b3", "n0", "n1", "a1"),
-    1: ("b4", "n2"),
-    3: ("b5", "n3", "n4", "a2"),
-    5: ("a3",),
-    "gated": ("bl", "a4"),
-    "passed 3": ("a5", "bd"),
+    "halo": ("y", "as", "b1"),
+    "sent": ("b2",),
+    "filter": ("b3",),
+    "signal": ("b4", "a1", "n0", "n1", "n2"),
+    1: ("b5", "n3", "n4"),
+    4: ("a2",),
+    "back": ("bl",),
+    "gated": ("a3",),
+    "passed 1": ("a4",),
+    "passed 2": ("a5", "bd"),
 }
 
 
@@ -71,17 +74,10 @@
     send[pl.ds(column // GROUP, width // GROUP)] = jnp.concatenate(parts, axis=1).astype(send.dtype)
 
 
-def unpack_channels(land, wide, out):
-    wide[...] = land[...].astype(jnp.float32).reshape(wide.shape)
-    blocks = out.shape[1]
-    for j in range(GROUP):
-        out[j] = wide[pl.ds(j, blocks, stride=GROUP), :]
-
-
 def block_kernel(
     scale, branches, taps, gain, long_filter, weight, out,
-    halo, extended, send_f, send_s, land_f, land_s, land_b, wide, gate, direct, signal, filters,
-    padded, filter_rows, shifted, total, weight_a, weight_b, gathered, product,
+    halo, extended, send_f, send_s, land_f, land_s, land_b, filters, signal, convolved, gate, direct,
+    padded, filter_rows, spread, tiles, partial, carried, weight_a, weight_b, gathered, product,
     round_sems, halo_sems, a2a_sems, y_sems, xa_send, xa_recv, za_send, za_recv, zb_send, zb_recv,
     xb_send, xb_recv, far_send, far_recv, back_recv, tp_send, tp_recv,
 ):
@@ -99,7 +95,8 @@
 
     x_peers = [at(z, lax.rem(x + t, nx), y) for t in range(1, nx)]
     z_peers = [at(lax.rem(z + t, nz), x, y) for t in range(1, nz)]
-    tp_peers = [{"tp": lax.rem(mine + t, tp_size)} for t in range(1, tp_size)]
+    tp_peers = [{"tp": mine + 1 - 2 * lax.rem(mine, 2)}]
+    tp_peers += [{"tp": lax.rem(mine + t, tp_size)} for t in (2, tp_size - 2)]
     other_y = at(z, x, 1 - y)
     following = {"seq": lax.rem(me + 1, seq_size)}
     leading = {"seq": lax.rem(me + seq_size - 1, seq_size)}
@@ -241,14 +238,14 @@
     weight_steps("sent")
     copy_f = scatter_wait(send_f, land_f, a2a_sems.at[0], a2a_sems.at[1])
     sent.append(copy_f)
-    unpack_channels(land_f, wide, filters)
     weight_steps("filter")
+    filters[...] = land_f[...].astype(jnp.float32).reshape(filters.shape)
     copy_s = scatter_wait(send_s, land_s, a2a_sems.at[2], a2a_sems.at[3])
-    unpack_channels(land_s, wide, signal)
     weight_steps("signal")
-    convolve(scale, signal, filters, padded, filter_rows, shifted, total, wide, pump)
+    signal[...] = land_s[...].astype(jnp.float32).reshape(signal.shape)
+    convolve(scale, signal, filters, padded, filter_rows, spread, tiles, partial, carried, convolved, pump)
     copy_s.wait_send()
-    send_s[...] = wide[...].reshape(send_s.shape).astype(send_s.dtype)
+    send_s[...] = convolved[...].reshape(send_s.shape).astype(send_s.dtype)
     parts = tp_send.shape[2]
     per_part = seq_size // parts
     my_part = me // per_part
@@ -343,7 +340,9 @@
     for t in range(1, chips):
         pass_on(t)
         weight_steps(f"passed {t}")
-    for t in range(chips):
+        if t == chips - 2:
+            add_all(0)
+    for t in range(1, chips):
         add_all(t)
     out[...] = product[...].astype(out.dtype)
 
@@ -364,55 +363,68 @@
             pl.when((i >= chip) & (chip > 0))(lambda: down(slot, k).wait_send())
 
 
-def convolve(scale, signal, long_filter, padded, taps, shifted, total, wide, midway):
-    blocks = signal.shape[1]
-    step = min(2 * SHIFTS, blocks)
-    padded[0:SHIFTS, :] = jnp.zeros((SHIFTS, LANES), jnp.float32)
+def convolve(scale, signal, long_filter, padded, taps, spread, tiles, partial, carried, out, midway):
+    blocks = signal.shape[0] // GROUP
+    groups = LANES // REACH
+    heads = 2 * groups
+    padded[0:TURN, :] = jnp.zeros((TURN, LANES), jnp.float32)
     taps[0:8, :] = jnp.zeros((8, LANES), jnp.float32)
-    row = lax.broadcasted_iota(jnp.int32, (LANES, LANES), 0)
-    lane = lax.broadcasted_iota(jnp.int32, (LANES, LANES), 1)
-    causal = lane >= row
+    carried[0:8, :] = jnp.zeros((8, LANES), jnp.float32)
+    lane = lax.broadcasted_iota(jnp.int32, (blocks, LANES), 1)
+    tile_row = lax.broadcasted_iota(jnp.int32, (TURN, LANES), 0)
+    tile_lane = lax.broadcasted_iota(jnp.int32, (TURN, LANES), 1)
 
     def rolled(block):
-        line = jnp.broadcast_to(taps[8 + block : 9 + block, :], (LANES, LANES))
+        line = jnp.broadcast_to(taps[8 + block : 9 + block, :], (TURN, LANES))
         return pltpu.roll(line, 0, 1, stride=1, stride_axis=0)
 
     def channel(j, carry):
         midway(j)
-        padded[SHIFTS:, :] = signal[j]
-        taps[8:, :] = long_filter[j]
-        for shift in range(SHIFTS):
-            shifted[:, shift * LANES : (shift + 1) * LANES] = padded[
-                SHIFTS - shift : SHIFTS - shift + blocks, :
-            ].astype(jnp.bfloat16)
-        for start in range(0, blocks, step):
+        padded[TURN:, :] = signal[pl.ds(j, blocks, stride=GROUP), :]
+        taps[8:, :] = long_filter[pl.ds(j, blocks, stride=GROUP), :]
+        for side in range(2):
+            turned = []
+            for v in range(groups):
+                head = groups * side + v
+                moved = padded[TURN - head : TURN - head + blocks, :].astype(jnp.bfloat16)
+                turned.append([pltpu.roll(moved, REACH * d, 1) if d else moved for d in range(groups)])
+            for i in range(groups):
+                tile = turned[0][-i % groups]
+                for v in range(1, groups):
+                    tile = jnp.where(lane >= REACH * v, turned[v][(v - i) % groups], tile)
+                spread[i, :, side * LANES : (side + 1) * LANES] = tile
+        last, last_low = rolled(-1), jnp.zeros((TURN, LANES), jnp.bfloat16)
+        for block in range(blocks):
+            here = rolled(block)
+            top = jnp.where(tile_lane >= tile_row, here, last).astype(jnp.bfloat16)
+            low = pltpu.roll(top, TURN, 1)
+            tail, head = block // heads, block % heads
+            tiles[tail // 2, head * REACH : (head + 1) * REACH, (tail % 2) * LANES : (tail % 2 + 1) * LANES] = (
+                jnp.concatenate([top, jnp.where(tile_lane >= TURN, low, last_low)], axis=0)
+            )
+            last, last_low = here, low
+        for pair in range(tiles.shape[0]):
+            start = 2 * heads * pair
             height = blocks - start
-            spans = range(start, min(start + step, blocks), SHIFTS)
-            last = [rolled(span - 1) for span in spans]
-            partial = None
-            for shift in range(0, SHIFTS, 2):
-                tiles = []
-                for extra in range(2):
-                    here = [rolled(span + shift + extra) for span in spans]
-                    tiles.append(
-                        jnp.concatenate(
-                            [jnp.where(causal, h, b).astype(jnp.bfloat16) for h, b in zip(here, last)], axis=1
-                        )
-                    )
-                    last = here
-                term = jnp.dot(
-                    shifted[0:height, shift * LANES : (shift + 2) * LANES],
-                    jnp.concatenate(tiles, axis=0),
-                    preferred_element_type=jnp.float32,
-                )
-                partial = term if partial is None else partial + term
-            if start == 0:
-                total[...] = partial[:, :LANES]
+            term = jnp.dot(
+                spread[:, 0:height, :].reshape(groups * height, 2 * LANES),
+                tiles[pair],
+                preferred_element_type=jnp.float32,
+            ).reshape(groups, height, 2 * LANES)
+            if pair == 0:
+                partial[...] = term[:, :, :LANES]
             else:
-                total[start:, :] += partial[:, :LANES]
-            if len(spans) > 1:
-                total[start + SHIFTS :, :] += partial[: height - SHIFTS, LANES:]
-        wide[pl.ds(j, blocks, stride=GROUP), :] = total[...] * scale
+                partial[:, start:, :] += term[:, :, :LANES]
+            partial[:, start + heads :, :] += term[:, : height - heads, LANES:]
+        stay, over = partial[0], None
+        for i in range(1, groups):
+            turned = pltpu.roll(partial[i], REACH * i, 1)
+            inside = lane >= REACH * i
+            stay += jnp.where(inside, turned, 0.0)
+            beyond = jnp.where(inside, 0.0, turned)
+            over = beyond if over is None else over + beyond
+        carried[8:, :] = over
+        out[pl.ds(j, blocks, stride=GROUP), :] = (stay + carried[7 : 7 + blocks, :]) * scale
         return carry
 
     lax.fori_loop(0, GROUP, channel, 0)
@@ -425,7 +437,7 @@
     assert channels == GROUP * seq_size and nz == tp_size and nx * ny * weight_rows == channels
     halves = rows // LANES
     blocks = halves * seq_size
-    columns_a = columns // 4
+    columns_a = columns // PART_A
     slots = (seq_size, halves * GROUP, LANES)
     f32, b16 = jnp.float32, jnp.bfloat16
     dma = pltpu.SemaphoreType.DMA
@@ -441,13 +453,14 @@
             pltpu.VMEM((3, 16, channels), b16),
             pltpu.VMEM((3, 16 + rows, min(LANES, channels)), f32),
             *[pltpu.VMEM(slots, b16)] * 5,
-            pltpu.VMEM((blocks * GROUP, LANES), f32),
+            *[pltpu.VMEM((blocks * GROUP, LANES), f32)] * 3,
             *[pltpu.VMEM((rows, channels), f32)] * 2,
-            *[pltpu.VMEM((GROUP, blocks, LANES), f32)] * 2,
-            pltpu.VMEM((SHIFTS + blocks, LANES), f32),
+            pltpu.VMEM((TURN + blocks, LANES), f32),
             pltpu.VMEM((8 + blocks, LANES), f32),
-            pltpu.VMEM((blocks, SHIFTS * LANES), b16),
-            pltpu.VMEM((blocks, LANES), f32),
+            pltpu.VMEM((LANES // REACH, blocks, 2 * LANES), b16),
+            pltpu.VMEM((blocks * REACH // (2 * LANES) // 2, 2 * LANES, 2 * LANES), b16),
+            pltpu.VMEM((LANES // REACH, blocks, LANES), f32),
+            pltpu.VMEM((8 + blocks, LANES), f32),
             pltpu.VMEM((nz, nx, ny, weight_rows, columns_a), b16),
             pltpu.VMEM((nx, nz, ny, weight_rows, columns - columns_a), b16),
             pltpu.VMEM((tp_size, rows, channels), b16),

time: 91.5 us -> 88.1 us (0.963)
  Pallas kernels: 86 us -> 82.6 us
    pallas_call x1, Pallas kernels: 86 us -> 82.6 us  [body(): pl.pallas_call(functools.partial(block_kernel, scale), out_shape=jax.Shap...]
where the time goes in v3:
time: 88.1 us; the launch traced here: 87.8 us
  Pallas kernels  82.6 us (94%)
  local copies, waits for them, and re-layouts  5.14 us (6%)
    pallas_call x1, Pallas kernels, body(): pl.pallas_call(functools.partial(block_kernel, scale), out_shape=jax.Shap...  82.6 us
    unnamed x11, local copies, waits for them, and re-layouts  5.14 us

profile of v3, /device:TPU:1, one launch (start us, length us, event | category | flops | bytes accessed | tf_op | source)
XLA Modules:
  0.0 87.8 jit_solution(10943040926741668788)
XLA Ops:
  0.0 0.0 copy-start
  0.0 1.1 %copy-done = bf16[3,256,512]{2,1,0:T(8,128)(2,1)S(1)} copy-done((bf16[3,256,512]{2,1,0:T(8,128)(2,1)S(1)}, bf16[3,256,512]{2,1,0:T(8,128)(2,1)}, u32[]{:S(2)}) %copy-start) | copy-done | bytes 786456
  1.1 0.0 copy-start.1
  1.1 1.0 %copy-done.1 = f32[256,512]{1,0:T(8,128)S(1)} copy-done((f32[256,512]{1,0:T(8,128)S(1)}, f32[256,512]{1,0:T(8,128)}, u32[]{:S(2)}) %copy-start.1) | copy-done | bytes 524312
  2.2 0.0 copy-start.2
  2.2 0.8 copy-done.2
  3.0 0.0 copy-start.3
  3.0 0.7 copy-done.3
  3.8 0.0 copy-start.4
  3.8 0.7 copy-done.4
  4.4 82.6 %hyena.1 = bf16[256,512]{1,0:T(8,128)(2,1)S(1)} custom-call(bf16[3,256,512]{2,1,0:T(8,128)(2,1)S(1)} %copy-done, f32[3,3,512]{2,1,0:T(4,128)S(1)} %copy-done.3, f32[1,512]{1,0:T(1,128)S(1)} %bitcast.1, f32[256,512]{1,0:T(8,128)S(1)} %copy-done.1, bf16[64,512]{1,0:T(8,128)(2,1)S(1)} %copy-done.2), custom_call_target="tpu_custom_call" | custom-call | tf_op jit(solution)/shard_map/hyena/pallas_call | solution.py:447
  87.0 0.7 copy.7
Async XLA Ops:
  0.0 1.1 %copy-start = (bf16[3,256,512]{2,1,0:T(8,128)(2,1)S(1)}, bf16[3,256,512]{2,1,0:T(8,128)(2,1)}, u32[]{:S(2)}) copy-start(bf16[3,256,512]{2,1,0:T(8,128)(2,1)} %branches.1) | copy-start | bytes 2359300
  1.1 1.0 %copy-start.1 = (f32[256,512]{1,0:T(8,128)S(1)}, f32[256,512]{1,0:T(8,128)}, u32[]{:S(2)}) copy-start(f32[256,512]{1,0:T(8,128)} %long_filter.1) | copy-start | bytes 1572868
  2.2 0.8 copy-start.2
  3.0 0.7 copy-start.3
  3.8 0.7 copy-start.4

commit v4 on v3

--- a/solution.py
+++ b/solution.py
@@ -13,16 +13,16 @@
 GROUP = 8
 REACH = 32
 TURN = 16
+UNROLL = 4
 PART_A = 2
 SCHEDULE = {
     "halo": ("y", "as", "b1"),
-    "sent": ("b2",),
+    "sent": ("b2", "n0"),
     "filter": ("b3",),
-    "signal": ("b4", "a1", "n0", "n1", "n2"),
-    1: ("b5", "n3", "n4"),
-    4: ("a2",),
-    "back": ("bl",),
-    "gated": ("a3",),
+    "signal": ("b4", "a1", "n1", "n2"),
+    3: ("b5", "n3", "n4"),
+    6: ("a2",),
+    "gated": ("a3", "bl"),
     "passed 1": ("a4",),
     "passed 2": ("a5", "bd"),
 }
@@ -58,7 +58,7 @@
         remote(send.at[peer], land.at[me], send_sem, recv_sem, {"seq": peer}).start()
         return carry
 
-    lax.fori_loop(1, count, step, 0)
+    lax.fori_loop(1, count, step, 0, unroll=UNROLL)
     land[me] = send[me]
 
 
@@ -69,9 +69,9 @@
     return copy
 
 
-def pack_rows(block_of, halves, send, column, width):
+def pack_rows(block_of, halves, send, slot, width):
     parts = [block_of(h).T.reshape(width // GROUP, GROUP, LANES) for h in range(halves)]
-    send[pl.ds(column // GROUP, width // GROUP)] = jnp.concatenate(parts, axis=1).astype(send.dtype)
+    send[pl.ds(slot, width // GROUP)] = jnp.concatenate(parts, axis=1).astype(send.dtype)
 
 
 def block_kernel(
@@ -110,7 +110,7 @@
     for column in range(0, channels, width):
         pack_rows(
             lambda h: long_filter[h * LANES : (h + 1) * LANES, column : column + width],
-            halves, send_f, column, width,
+            halves, send_f, column // GROUP, width,
         )
     pl.semaphore_wait(barrier, len(greeted))
     for peer in x_peers:
@@ -219,8 +219,21 @@
     halo_copy.wait()
     weight_steps("halo")
     first = me == 0
-    for column in range(0, channels, width):
-        span = slice(column, column + width)
+    parts = tp_send.shape[2]
+    per_part = seq_size // parts
+    my_part = me // per_part
+
+    def part_start(k, send, land, send_sem, recv_sem):
+        def step(i, carry):
+            peer = lax.rem(my_part + k, parts) * per_part + lax.rem(me + i, per_part)
+            remote(send.at[peer], land.at[me], send_sem, recv_sem, {"seq": peer}).start()
+            return carry
+
+        lax.fori_loop(1 if k == 0 else 0, per_part, step, 0, unroll=UNROLL)
+
+    for k in range(parts):
+        part = lax.rem(my_part + k, parts)
+        span = pl.ds(pl.multiple_of(part * width, width), width)
         mixed = []
         for branch in range(3):
             before = halo[branch, :, span].astype(jnp.float32)
@@ -233,8 +246,9 @@
         made = mixed[1] * mixed[2]
         gate[:, span] = mixed[0]
         direct[:, span] = gain[0:1, span] * made
-        pack_rows(lambda h: made[h * LANES : (h + 1) * LANES], halves, send_s, column, width)
-    scatter_start(send_s, land_s, a2a_sems.at[2], a2a_sems.at[3])
+        pack_rows(lambda h: made[h * LANES : (h + 1) * LANES], halves, send_s, part * per_part, width)
+        part_start(k, send_s, land_s, a2a_sems.at[2], a2a_sems.at[3])
+    land_s[me] = send_s[me]
     weight_steps("sent")
     copy_f = scatter_wait(send_f, land_f, a2a_sems.at[0], a2a_sems.at[1])
     sent.append(copy_f)
@@ -246,21 +260,11 @@
     convolve(scale, signal, filters, padded, filter_rows, spread, tiles, partial, carried, convolved, pump)
     copy_s.wait_send()
     send_s[...] = convolved[...].reshape(send_s.shape).astype(send_s.dtype)
-    parts = tp_send.shape[2]
-    per_part = seq_size // parts
-    my_part = me // per_part
-
     def part_at(k):
         return lax.rem(my_part + parts - k, parts)
 
     for k in range(parts):
-
-        def send_back(i, carry):
-            peer = lax.rem(my_part + k, parts) * per_part + lax.rem(me + i, per_part)
-            remote(send_s.at[peer], land_b.at[me], a2a_sems.at[4], back_recv.at[my_part], {"seq": peer}).start()
-            return carry
-
-        lax.fori_loop(1 if k == 0 else 0, per_part, send_back, 0)
+        part_start(k, send_s, land_b, a2a_sems.at[4], back_recv.at[my_part])
     land_b[me] = send_s[me]
     sent.append(remote(send_s.at[pl.ds(1, seq_size - 1)], land_b.at[pl.ds(1, seq_size - 1)], a2a_sems.at[4], a2a_sems.at[5], other_y))
     weight_steps("back")

time: 88.1 us -> 85.7 us (0.973)
  Pallas kernels: 82.6 us -> 80.2 us
    pallas_call x1, Pallas kernels: 82.6 us -> 80.2 us  [body(): pl.pallas_call(functools.partial(block_kernel, scale), out_shape=jax.Shap...]
where the time goes in v4:
time: 85.7 us; the launch traced here: 85.4 us
  Pallas kernels  80.2 us (94%)
  local copies, waits for them, and re-layouts  5.14 us (6%)
    pallas_call x1, Pallas kernels, body(): pl.pallas_call(functools.partial(block_kernel, scale), out_shape=jax.Shap...  80.2 us
    unnamed x11, local copies, waits for them, and re-layouts  5.14 us

profile of v4, /device:TPU:1, one launch (start us, length us, event | category | flops | bytes accessed | tf_op | source)
XLA Modules:
  0.0 85.4 jit_solution(8823165880361015190)
XLA Ops:
  0.0 0.0 copy-start
  0.0 1.1 %copy-done = bf16[3,256,512]{2,1,0:T(8,128)(2,1)S(1)} copy-done((bf16[3,256,512]{2,1,0:T(8,128)(2,1)S(1)}, bf16[3,256,512]{2,1,0:T(8,128)(2,1)}, u32[]{:S(2)}) %copy-start) | copy-done | bytes 786456
  1.1 0.0 copy-start.1
  1.1 1.0 %copy-done.1 = f32[256,512]{1,0:T(8,128)S(1)} copy-done((f32[256,512]{1,0:T(8,128)S(1)}, f32[256,512]{1,0:T(8,128)}, u32[]{:S(2)}) %copy-start.1) | copy-done | bytes 524312
  2.2 0.0 copy-start.2
  2.2 0.8 copy-done.2
  3.0 0.0 copy-start.3
  3.0 0.7 copy-done.3
  3.8 0.0 copy-start.4
  3.8 0.7 copy-done.4
  4.4 80.2 %hyena.1 = bf16[256,512]{1,0:T(8,128)(2,1)S(1)} custom-call(bf16[3,256,512]{2,1,0:T(8,128)(2,1)S(1)} %copy-done, f32[3,3,512]{2,1,0:T(4,128)S(1)} %copy-done.3, f32[1,512]{1,0:T(1,128)S(1)} %bitcast.1, f32[256,512]{1,0:T(8,128)S(1)} %copy-done.1, bf16[64,512]{1,0:T(8,128)(2,1)S(1)} %copy-done.2), custom_call_target="tpu_custom_call" | custom-call | tf_op jit(solution)/shard_map/hyena/pallas_call | solution.py:451
  84.6 0.7 copy.7
Async XLA Ops:
  0.0 1.1 %copy-start = (bf16[3,256,512]{2,1,0:T(8,128)(2,1)S(1)}, bf16[3,256,512]{2,1,0:T(8,128)(2,1)}, u32[]{:S(2)}) copy-start(bf16[3,256,512]{2,1,0:T(8,128)(2,1)} %branches.1) | copy-start | bytes 2359300
  1.1 1.0 %copy-start.1 = (f32[256,512]{1,0:T(8,128)S(1)}, f32[256,512]{1,0:T(8,128)}, u32[]{:S(2)}) copy-start(f32[256,512]{1,0:T(8,128)} %long_filter.1) | copy-start | bytes 1572868
  2.2 0.8 copy-start.2
  3.0 0.7 copy-start.3
  3.8 0.7 copy-start.4

commit v5 on v4

--- a/solution.py
+++ b/solution.py
@@ -346,7 +346,8 @@
         weight_steps(f"passed {t}")
         if t == chips - 2:
             add_all(0)
-    for t in range(1, chips):
+            add_all(1)
+    for t in range(2, chips):
         add_all(t)
     out[...] = product[...].astype(out.dtype)
 

time: 85.7 us -> 86.1 us (level)
  no operation moved by 1% of the time
where the time goes in v5:
time: 86.1 us; the launch traced here: 85.8 us
  Pallas kernels  80.6 us (94%)
  local copies, waits for them, and re-layouts  5.14 us (6%)
    pallas_call x1, Pallas kernels, body(): pl.pallas_call(functools.partial(block_kernel, scale), out_shape=jax.Shap...  80.6 us
    unnamed x11, local copies, waits for them, and re-layouts  5.14 us

profile of v5, /device:TPU:1, one launch (start us, length us, event | category | flops | bytes accessed | tf_op | source)
XLA Modules:
  0.0 85.8 jit_solution(2965737723278201680)
XLA Ops:
  0.0 0.0 copy-start
  0.0 1.1 %copy-done = bf16[3,256,512]{2,1,0:T(8,128)(2,1)S(1)} copy-done((bf16[3,256,512]{2,1,0:T(8,128)(2,1)S(1)}, bf16[3,256,512]{2,1,0:T(8,128)(2,1)}, u32[]{:S(2)}) %copy-start) | copy-done | bytes 786456
  1.1 0.0 copy-start.1
  1.1 1.0 %copy-done.1 = f32[256,512]{1,0:T(8,128)S(1)} copy-done((f32[256,512]{1,0:T(8,128)S(1)}, f32[256,512]{1,0:T(8,128)}, u32[]{:S(2)}) %copy-start.1) | copy-done | bytes 524312
  2.2 0.0 copy-start.2
  2.2 0.8 copy-done.2
  3.0 0.0 copy-start.3
  3.0 0.7 copy-done.3
  3.8 0.0 copy-start.4
  3.8 0.7 copy-done.4
  4.4 80.6 %hyena.1 = bf16[256,512]{1,0:T(8,128)(2,1)S(1)} custom-call(bf16[3,256,512]{2,1,0:T(8,128)(2,1)S(1)} %copy-done, f32[3,3,512]{2,1,0:T(4,128)S(1)} %copy-done.3, f32[1,512]{1,0:T(1,128)S(1)} %bitcast.1, f32[256,512]{1,0:T(8,128)S(1)} %copy-done.1, bf16[64,512]{1,0:T(8,128)(2,1)S(1)} %copy-done.2), custom_call_target="tpu_custom_call" | custom-call | tf_op jit(solution)/shard_map/hyena/pallas_call | solution.py:452
  85.1 0.7 copy.7
Async XLA Ops:
  0.0 1.1 %copy-start = (bf16[3,256,512]{2,1,0:T(8,128)(2,1)S(1)}, bf16[3,256,512]{2,1,0:T(8,128)(2,1)}, u32[]{:S(2)}) copy-start(bf16[3,256,512]{2,1,0:T(8,128)(2,1)} %branches.1) | copy-start | bytes 2359300
  1.1 1.0 %copy-start.1 = (f32[256,512]{1,0:T(8,128)S(1)}, f32[256,512]{1,0:T(8,128)}, u32[]{:S(2)}) copy-start(f32[256,512]{1,0:T(8,128)} %long_filter.1) | copy-start | bytes 1572868
  2.2 0.8 copy-start.2
  3.0 0.7 copy-start.3
  3.8 0.7 copy-start.4
